TPU v7x, 32 devices: a whole 2x2x4 slice. The times are simulated.
32 devices in a mesh: ctx: 16 (over z, x, core), heads: 2 (over y).
Axes of the slice: x: 2, y: 2, z: 4, core: 2. Of those that a mesh axis runs over, the one named last changes fastest.
Arguments:
- hidden: bfloat16 [8192, 5376], P(('ctx', 'heads')), may hold values from -8 to 8
- query_weight: bfloat16 [5376, 2048], P(None, 'heads'), may hold values from -0.5 to 0.5
- key_weight: bfloat16 [5376, 1024], P(None, 'heads'), may hold values from -0.5 to 0.5
- value_weight: bfloat16 [5376, 1024], P(None, 'heads'), may hold values from -0.078125 to 0.078125
- query_gain: float32 [128], replicated, may hold values from 0.5 to 6
- key_gain: float32 [128], replicated, may hold values from 0.5 to 6
- out_grad: bfloat16 [8192, 2048], P('ctx', 'heads'), may hold values from -6 to 6
Outputs:
- attention: bfloat16 [8192, 2048], P('ctx', 'heads')
- input_grad: bfloat16 [8192, 5376], P(('ctx', 'heads'))
- query_weight_grad: float32 [5376, 2048], P('ctx', 'heads')
- key_weight_grad: float32 [5376, 1024], P('ctx', 'heads')
- value_weight_grad: float32 [5376, 1024], P('ctx', 'heads')
All inputs are finite; a program needn't handle non-finite values.
Results may differ from a plain program's by a relative error of at most 0.039.
Values may be sent and summed in bfloat16 or wider, within the bound.
A program may use at most 192 MiB of HBM per device.

v0:
```python
import math

import jax
import jax.numpy as jnp
from jax import lax
from jax.sharding import PartitionSpec as P

HEAD_DIM = 128
WINDOW = 1024
SCALAR = 168
HEADS = 16
KV_HEADS = 8


def passed_along(block, axis, distance):
    devices = range(lax.axis_size(axis))
    route = [(i - distance, i) for i in devices if i - distance in devices]
    return lax.ppermute(block, axis, route)


def rope_tables(positions, head_size):
    half_size = head_size // 2
    indices = jnp.arange(half_size, dtype=jnp.float32)
    inverse = jnp.exp(indices * (-2.0 * math.log(10000.0) / head_size))
    angles = positions.astype(jnp.float32)[:, None] * inverse[None, :]
    return (jnp.cos(angles), jnp.sin(angles))


def prepare(projected, cosine, sine_table, channel_gain, factor):
    row_count = projected.shape[0]
    head_size = channel_gain.shape[0]
    pieces = projected.reshape(row_count, -1, head_size)
    normed = (
        pieces * lax.rsqrt(jnp.mean(pieces * pieces, axis=-1, keepdims=True) + 1e-06) * channel_gain
    )
    half_size = head_size // 2
    leading = normed[..., :half_size]
    trailing = normed[..., half_size:]
    cos_rows = cosine[:, None, :]
    sin_rows = sine_table[:, None, :]
    turned = jnp.concatenate(
        [leading * cos_rows - trailing * sin_rows, trailing * cos_rows + leading * sin_rows],
        axis=-1,
    )
    return (turned * factor).reshape(row_count, -1)


def band_mask(query_pos, key_pos):
    separation = query_pos[:, None] - key_pos[None, :]
    return (separation >= 0) & (separation < WINDOW) & (key_pos[None, :] >= 0)


def head_grids(query_block, key_window, value_window, group_size):
    query_grid = query_block.reshape(query_block.shape[0], -1, group_size, HEAD_DIM)
    key_grid = key_window.reshape(key_window.shape[0], -1, HEAD_DIM)
    value_grid = value_window.reshape(value_window.shape[0], -1, HEAD_DIM)
    return (query_grid, key_grid, value_grid)


def attend_forward(query_block, key_window, value_window, allowed, group_size):
    query_grid, key_grid, value_grid = head_grids(query_block, key_window, value_window, group_size)
    scores = jnp.einsum("qkgd,jkd->kgqj", query_grid, key_grid, preferred_element_type=jnp.float32)
    masked = jnp.where(allowed, scores, -1e30)
    highest = jnp.max(masked, axis=-1, keepdims=True)
    total = jnp.sum(jnp.exp(masked - highest), axis=-1, keepdims=True)
    log_total = highest + jnp.log(total)
    weights = jnp.where(allowed, jnp.exp(masked - log_total), 0.0)
    output = jnp.einsum(
        "kgqj,jkd->qkgd",
        weights.astype(jnp.bfloat16),
        value_grid,
        preferred_element_type=jnp.float32,
    )
    return (output.reshape(query_block.shape[0], -1), log_total[..., 0])


def attend_backward(
    query_block,
    key_window,
    value_window,
    allowed,
    log_total,
    out_block,
    attention_block,
    group_size,
):
    query_grid, key_grid, value_grid = head_grids(query_block, key_window, value_window, group_size)
    row_count = query_block.shape[0]
    grad_grid = out_block.reshape(row_count, -1, group_size, HEAD_DIM)
    attention_grid = attention_block.reshape(row_count, -1, group_size, HEAD_DIM)
    scores = jnp.einsum("qkgd,jkd->kgqj", query_grid, key_grid, preferred_element_type=jnp.float32)
    masked = jnp.where(allowed, scores, -1e30)
    weights = jnp.where(allowed, jnp.exp(masked - log_total[..., None]), 0.0)
    delta = jnp.einsum(
        "qkgd,qkgd->kgq", grad_grid, attention_grid, preferred_element_type=jnp.float32
    )
    products = jnp.einsum(
        "qkgd,jkd->kgqj", grad_grid, value_grid, preferred_element_type=jnp.float32
    )
    shifts = (weights * (products - delta[..., None])).astype(jnp.bfloat16)
    query_cot = jnp.einsum(
        "kgqj,jkd->qkgd", shifts, key_grid, preferred_element_type=jnp.float32
    ).reshape(row_count, -1)
    key_cot = jnp.einsum(
        "kgqj,qkgd->jkd", shifts, query_grid, preferred_element_type=jnp.float32
    ).reshape(key_window.shape[0], -1)
    value_cot = jnp.einsum(
        "kgqj,qkgd->jkd",
        weights.astype(jnp.bfloat16),
        grad_grid,
        preferred_element_type=jnp.float32,
    ).reshape(key_window.shape[0], -1)
    return (query_cot, key_cot, value_cot)


def per_device(hidden, query_weight, key_weight, value_weight, query_gain, key_gain, out_grad):
    token_count = out_grad.shape[0]
    group_size = HEADS // KV_HEADS
    block_rows = min(token_count, 512)
    block_count = token_count // block_rows
    window_rows = block_rows + WINDOW
    reach_blocks = (WINDOW - 2) // token_count + 1
    position_base = lax.axis_index("ctx") * token_count
    gathered = lax.all_gather(hidden, "heads", axis=0, tiled=True)
    query_proj = jnp.dot(gathered, query_weight, preferred_element_type=jnp.float32)
    key_proj = jnp.dot(gathered, key_weight, preferred_element_type=jnp.float32)
    value_proj = jnp.dot(gathered, value_weight, preferred_element_type=jnp.float32)
    positions = position_base + jnp.arange(token_count, dtype=jnp.int32)
    cosine, sine_table = rope_tables(positions, HEAD_DIM)
    query_full, query_back = jax.vjp(
        lambda projected: prepare(projected, cosine, sine_table, query_gain, SCALAR ** (-0.5)),
        query_proj,
    )
    key_full, key_back = jax.vjp(
        lambda projected: prepare(projected, cosine, sine_table, key_gain, 1.0), key_proj
    )
    query_cast = query_full.astype(jnp.bfloat16)
    key_value = jnp.stack([key_full.astype(jnp.bfloat16), value_proj.astype(jnp.bfloat16)])
    received = [passed_along(key_value, "ctx", distance) for distance in range(1, reach_blocks + 1)]
    window_pair = jnp.concatenate(received[::-1] + [key_value], axis=1)
    key_span = window_pair[0]
    value_span = window_pair[1]

    def window_of(block_index):
        block_start = block_index * block_rows
        query_pos = position_base + block_start + jnp.arange(block_rows, dtype=jnp.int32)
        key_pos = position_base - WINDOW + block_start + jnp.arange(window_rows, dtype=jnp.int32)
        return (query_cast, key_span, value_span, band_mask(query_pos, key_pos))

    def forward_block(block_index):
        query_block, key_window, value_window, allowed = window_of(block_index)
        return attend_forward(query_block, key_window, value_window, allowed, group_size)

    outputs, log_totals = lax.map(forward_block, jnp.arange(block_count, dtype=jnp.int32))
    attention = outputs.reshape(token_count, -1).astype(jnp.bfloat16)

    def backward_block(block_index, carry):
        query_acc, pair_acc = carry
        query_block, key_window, value_window, allowed = window_of(block_index)
        block_start = block_index * block_rows
        query_cot, key_cot, value_cot = attend_backward(
            query_block,
            key_window,
            value_window,
            allowed,
            log_totals[block_index],
            out_grad,
            attention,
            group_size,
        )
        query_acc = query_cot
        region = pair_acc + jnp.stack([key_cot, value_cot])
        pair_acc = region
        return (query_acc, pair_acc)

    query_zero = jnp.zeros((token_count, query_weight.shape[1]), jnp.float32)
    pair_zero = jnp.zeros((2, (reach_blocks + 1) * token_count, key_weight.shape[1]), jnp.float32)
    query_acc, pair_acc = lax.fori_loop(0, block_count, backward_block, (query_zero, pair_zero))
    grad_query = query_back(query_acc)[0].astype(jnp.bfloat16)
    grad_scale = float(lax.axis_size("ctx") * token_count) ** (-0.5)
    contract = (((0,), (0,)), ((), ()))
    own_pair = pair_acc[:, reach_blocks * token_count :]
    for distance in range(1, reach_blocks + 1):
        lower_row = (reach_blocks - distance) * token_count
        own_pair = own_pair + passed_along(
            pair_acc[:, lower_row : lower_row + token_count], "ctx", -distance
        )
    grad_key = key_back(own_pair[0])[0].astype(jnp.bfloat16)
    grad_value = own_pair[1].astype(jnp.bfloat16)
    key_width = key_weight.shape[1]
    query_width = query_weight.shape[1]
    summed = lax.psum_scatter(
        (
            lax.dot_general(
                gathered,
                jnp.concatenate([grad_query, grad_key, grad_value], axis=1),
                contract,
                preferred_element_type=jnp.float32,
            )
            * grad_scale
        ).astype(jnp.bfloat16),
        "ctx",
        scatter_dimension=0,
        tiled=True,
    ).astype(jnp.float32)
    query_weight_grad = summed[:, :query_width]
    key_weight_grad = summed[:, query_width : query_width + key_width]
    value_weight_grad = summed[:, query_width + key_width :]
    back_contract = (((1,), (1,)), ((), ()))
    partial_sum = lax.dot_general(
        grad_query, query_weight, back_contract, preferred_element_type=jnp.float32
    )
    partial_sum = partial_sum + lax.dot_general(
        grad_key, key_weight, back_contract, preferred_element_type=jnp.float32
    )
    input_grad = lax.psum_scatter(
        (
            partial_sum
            + lax.dot_general(
                grad_value, value_weight, back_contract, preferred_element_type=jnp.float32
            )
        ).astype(jnp.bfloat16),
        "heads",
        scatter_dimension=0,
        tiled=True,
    )
    return (attention, input_grad, query_weight_grad, key_weight_grad, value_weight_grad)


def solution(mesh):
    return jax.shard_map(
        per_device,
        mesh=mesh,
        in_specs=(
            P(("ctx", "heads"), None),
            P(None, "heads"),
            P(None, "heads"),
            P(None, "heads"),
            P(),
            P(),
            P("ctx", "heads"),
        ),
        out_specs=(
            P("ctx", "heads"),
            P(("ctx", "heads"), None),
            P("ctx", "heads"),
            P("ctx", "heads"),
            P("ctx", "heads"),
        ),
        check_vma=False,
    )
```

profile of v0, /device:TPU:0, one launch (start us, length us, event | category | flops | bytes accessed | tf_op | source)
XLA Modules:
  0.0 672.1 jit_solution(1559258074041350741)
XLA Ops:
  8.0 1.0 multiply_cosine_fusion
  10.7 2.5 copy.103
  13.2 1.2 fusion.6
  14.4 69.4 %all-gather.2.cloned.1.call-done = bf16[512,5376]{1,0:T(8,128)(2,1)} async-done(((bf16[256,5376]{1,0:T(8,128)(2,1)}), bf16[512,5376]{1,0:T(8,128)(2,1)}) %all-gather.2.cloned.1.call-update) | async-done | bytes 5505040 | tf_op jit(solution)/shard_map/all_gather | solution.py:124
  83.8 6.7 %multiply_reduce_fusion.4 = (f32[512,4]{0,1:T(4,128)S(1)}, f32[512,512]{0,1:T(8,128)S(1)}) fusion(bf16[512,5376]{1,0:T(8,128)(2,1)} %all-gather.2.cloned.1.call-done, bf16[5376,512]{1,0:T(8,128)(2,1)} %param.9), kind=kOutput, calls=%fused_computation.59 | convolution fusion | flops 2819094528 | bytes 12066816 | tf_op jit(solution)/shard_map/dot_general | solution.py:126
  90.6 0.9 copy-done.7
  92.2 7.3 %fusion.20 = bf16[1,512,512]{2,1,0:T(8,128)(2,1)S(1)} fusion(bf16[512,5376]{1,0:T(8,128)(2,1)} %all-gather.2.cloned.1.call-done, bf16[5376,512]{1,0:T(8,128)(2,1)} %param.10), kind=kOutput, calls=%fused_computation.50 | convolution fusion | flops 2818834432 | bytes 11534336 | tf_op jit(solution)/shard_map/dot_general | solution.py:127
  99.6 1.1 pad_maximum_fusion.1
  100.7 2.7 collective-permute-start.1
  103.4 4.1 collective-permute-start
  107.5 8.6 %convolution_bitcast_fusion = f32[64,8,8,128]{3,1,2,0:T(8,128)S(1)} fusion(bf16[512,5376]{1,0:T(8,128)(2,1)S(1)} %bitcast.126, bf16[5376,1024]{1,0:T(8,128)(2,1)} %param.8), kind=kOutput, calls=%fused_computation.44 | convolution fusion | flops 5637144576 | bytes 18612224 | tf_op jit(solution)/shard_map/dot_general | solution.py:125
  116.6 1.3 multiply_reduce_fusion.2
  117.9 1.0 copy.86
  119.6 1.6 copy.87
  121.1 1.7 multiply_multiply_fusion
  122.8 1.1 multiply_subtract_fusion
  124.5 1.1 copy.88
  125.7 4.2 collective-permute-done
  129.9 1.7 maximum_maximum_fusion
  131.7 1.9 fusion.31
  133.6 3.5 reshape_squeeze.16
  137.1 3.8 copy.121
  140.9 3.5 reshape_squeeze.15
  144.4 13.8 %fusion.2 = (f32[4,2,512]{2,1,0:T(2,128)S(1)}, f32[4,1536,512,2]{2,1,3,0:T(8,128)}) fusion(pred[512,1536]{0,1:T(8,128)(4,1)S(1)} %fusion.6, bf16[1536,4,128,1]{0,2,3,1:T(8,128)(2,1)} %copy.121, bf16[512,4,2,128]{3,0,2,1:T(8,128)(2,1)} %bitcast.106), kind=kOutput, calls=%fused_computation.7 | convolution fusion | flops 1623191552 | bytes 28590080 | tf_op jit(solution)/shard_map/while/body/eval_jaxpr/qkgd,jkd->kgqj/dot_general | solution.py:62
  158.2 10.8 %exponential_reduce_fusion = f32[4,2,512]{2,1,0:T(2,128)S(1)} fusion(f32[4,1536,512,2]{2,1,3,0:T(8,128)} %get-tuple-element.99, f32[4,2,512]{2,1,0:T(2,128)S(1)} %get-tuple-element.98, pred[512,1536]{0,1:T(8,128)(4,1)S(1)} %fusion.6), kind=kLoop, calls=%fused_computation.6 | loop fusion | flops 18870272 | bytes 25985024 | tf_op jit(solution)/shard_map/while/body/eval_jaxpr/reduce_sum | solution.py:65
  169.0 13.4 %fusion.27 = f32[4,1536,128,1]{1,2,3,0:T(8,128)} fusion(bf16[512,4,2,128]{0,3,2,1:T(8,128)(2,1)S(1)} %copy-done.26, f32[4,1536,512,2]{2,1,3,0:T(8,128)} %get-tuple-element.99, f32[4,2,512]{2,1,0:T(2,128)S(1)} %bitcast.122, pred[512,1536]{0,1:T(8,128)(4,1)S(1)} %fusion.6), kind=kOutput, calls=%fused_computation.81 | convolution fusion | flops 1635778560 | bytes 30162944 | tf_op jit(solution)/shard_map/while/body/eval_jaxpr/kgqj,qkgd->jkd/dot_general | solution.py:107
  182.3 13.2 %bitcast_convert_fusion = (f32[4,2,512,128]{2,3,1,0:T(8,128)}, bf16[4,128,2,512]{3,1,2,0:T(8,128)(2,1)}) fusion(f32[4,1536,512,2]{2,1,3,0:T(8,128)} %get-tuple-element.99, f32[4,2,512]{2,1,0:T(2,128)S(1)} %bitcast.123, pred[512,1536]{0,1:T(8,128)(4,1)S(1)} %fusion.6, bf16[1536,4,128,1]{2,1,0,3:T(4,128)(2,1)S(1)} %bitcast.117), kind=kOutput, calls=%fused_computation.55 | convolution fusion | flops 1636827136 | bytes 30687232 | tf_op jit(solution)/shard_map/while/body/eval_jaxpr/kgqj,jkd->qkgd/dot_general | solution.py:68
  195.5 4.1 copy.119
  199.7 5.4 multiply_reduce_fusion
  205.0 1.6 copy.120
  206.6 16.1 %fusion.1 = bf16[4,2,512,1536]{2,3,1,0:T(8,128)(2,1)} fusion(f32[4,1536,512,2]{2,1,3,0:T(8,128)} %get-tuple-element.99, bf16[512,4,2,128]{0,3,2,1:T(8,128)(2,1)} %copy.103, f32[4,2,512]{2,1,0:T(2,128)S(1)} %copy.120, f32[4,2,512]{2,1,0:T(2,128)S(1)} %bitcast.124, pred[512,1536]{0,1:T(8,128)(4,1)S(1)} %fusion.6, bf16[1536,4,128,1]{2,1,0,3:T(4,128)(2,1)} %bitcast.116), kind=kOutput, calls=%fused_computation.3 | convolution fusion | flops 1648361472 | bytes 41189376 | tf_op jit(solution)/shard_map/while/body/eval_jaxpr/qkgd,jkd->kgqj/dot_general | solution.py:97
  222.7 9.3 %fusion.35 = f32[4,128,1536,1]{2,1,3,0:T(8,128)S(1)} fusion(bf16[512,4,2,128]{3,0,2,1:T(8,128)(2,1)} %bitcast.107, bf16[4,2,512,1536]{2,3,1,0:T(8,128)(2,1)} %fusion.1), kind=kOutput, calls=%fused_computation.86 | convolution fusion | flops 1610612736 | bytes 16777216 | tf_op jit(solution)/shard_map/while/body/eval_jaxpr/kgqj,qkgd->jkd/dot_general | solution.py:104
  232.0 2.5 fusion.8
  235.0 1.3 collective-permute-start.2
  236.3 1.3 collective-permute-start.3
  237.6 6.4 convolution_multiply_fusion
  244.0 1.6 fusion.32
  245.6 3.3 copy.141
  248.9 3.2 copy.142
  252.1 2.7 multiply_add_fusion.1
  254.8 1.4 copy-done.2
  256.8 1.2 multiply_reduce_fusion.1
  258.3 4.6 fusion.7
  262.9 1.3 copy.153
  264.3 52.3 %collective-permute-done.3 = f32[2,512,512]{1,2,0:T(8,128)} collective-permute-done((f32[2,512,512]{1,2,0:T(8,128)}, f32[2,512,512]{1,2,0:T(8,128)}, u32[]{:S(2)}, u32[]{:S(2)}) %collective-permute-start.3) | collective-permute-done | bytes 2097184 | tf_op jit(solution)/shard_map/ppermute | solution.py:18
  316.6 3.0 fusion.11
  320.4 1.0 slice.67
  321.5 2.1 copy.105
  323.6 1.4 multiply_add_fusion.4
  325.2 1.1 fusion.21
  326.3 1.3 copy.104
  327.6 19.0 %fusion.3 = bf16[5376,2048]{0,1:T(8,128)(2,1)} fusion(bf16[512,5376]{1,0:T(8,128)(2,1)} %all-gather.2.cloned.1.call-done, bf16[512,512]{1,0:T(8,128)(2,1)} %copy.105, bf16[512,512]{1,0:T(8,128)(2,1)S(1)} %copy.104, bf16[512,1024]{1,0:T(8,128)(2,1)} %bitcast.119), kind=kOutput, calls=%fused_computation.8 | convolution fusion | flops 11302600704 | bytes 29622272 | tf_op jit(solution)/shard_map/dot_general | solution.py:194
  346.6 28.7 %copy.139 = bf16[5376,2048]{1,0:T(8,128)(2,1)} copy(bf16[5376,2048]{0,1:T(8,128)(2,1)} %fusion.3) | data formatting | bytes 44040192
  375.4 14.0 %fusion.30 = f32[512,5376]{1,0:T(8,128)} fusion(bf16[5376,1024]{1,0:T(8,128)(2,1)} %param.8, bf16[64,8,8,128]{3,2,1,0:T(8,128)(2,1)} %bitcast.113), kind=kOutput, calls=%fused_computation.82 | convolution fusion | flops 5637144576 | bytes 23068672 | tf_op jit(solution)/shard_map/dot_general | solution.py:210
  389.5 11.8 %fusion.36 = f32[512,5376]{1,0:T(8,128)} fusion(bf16[512,512]{0,1:T(8,128)(2,1)S(1)} %bitcast.111, bf16[5376,512]{1,0:T(8,128)(2,1)} %param.9), kind=kOutput, calls=%fused_computation.87 | convolution fusion | flops 2818572288 | bytes 17039360 | tf_op jit(solution)/shard_map/dot_general | solution.py:213
  401.3 15.1 %add_convert_fusion = bf16[512,5376]{1,0:T(8,128)(2,1)} fusion(f32[512,5376]{1,0:T(8,128)} %fusion.30, f32[512,5376]{1,0:T(8,128)} %fusion.36, bf16[5376,512]{1,0:T(8,128)(2,1)} %param.10, f32[2,512,512]{1,2,0:T(8,128)S(1)} %fusion.11), kind=kOutput, calls=%fused_computation.10 | convolution fusion | flops 2826829824 | bytes 33554432 | tf_op jit(solution)/shard_map/dot_general | solution.py:219
  416.4 1.5 copy-done.25
  418.0 1.3 copy.106
  419.3 175.6 %reduce-scatter.7.cloned.1.call-done = bf16[336,2048]{1,0:T(8,128)(2,1)} async-done(((bf16[5376,2048]{1,0:T(8,128)(2,1)}), bf16[336,2048]{1,0:T(8,128)(2,1)}) %reduce-scatter.7.cloned.1.call-update) | async-done | bytes 1376272
  594.9 1.8 copy.140
  596.8 1.5 copy.107
  598.5 1.1 copy.109
  599.6 1.1 copy.108
  600.7 64.7 %reduce-scatter.5.cloned.1.call-done = bf16[256,5376]{1,0:T(8,128)(2,1)} async-done(((bf16[512,5376]{1,0:T(8,128)(2,1)}), bf16[256,5376]{1,0:T(8,128)(2,1)}) %reduce-scatter.5.cloned.1.call-update) | async-done | bytes 2752528 | tf_op jit(solution)/shard_map/reduce_scatter | solution.py:216
  (102 shorter events, 7.7 us)
Async XLA Ops:
  7.2 2.7 copy-start.24
  7.2 76.6 %all-gather.2.cloned.1.call-start = ((), (), s32[]{:S(2)}) async-start(), calls=%async_computation.2 | async-start | bytes 8257536 | tf_op jit(solution)/shard_map/all_gather | solution.py:124
  7.9 587.0 %reduce-scatter.7.cloned.1.call-start = ((), (), s32[]{:S(2)}) async-start(), calls=%async_computation.4 | async-start | bytes 23396352
  9.0 0.7 copy-start.11
  9.0 0.8 copy-start.14
  9.9 81.8 %copy-start.22 = (f32[512,64]{0,1:T(8,128)}, f32[512,64]{0,1:T(8,128)S(1)}, u32[]{:S(2)}) copy-start(f32[512,64]{0,1:T(8,128)S(1)} %copy.84) | copy-start | bytes 393220
  10.7 79.8 %copy-start.9 = (bf16[512,4,2,128]{3,2,1,0:T(2,128)(2,1)}, bf16[512,4,2,128]{3,2,1,0:T(2,128)(2,1)S(1)}, u32[]{:S(2)}) copy-start(bf16[512,4,2,128]{3,2,1,0:T(2,128)(2,1)S(1)} %reshape.198) | copy-start | bytes 3145732
  14.4 77.2 %copy-start.31 = (f32[128]{0:T(128)S(1)}, f32[128]{0:T(128)}, u32[]{:S(2)}) copy-start(f32[128]{0:T(128)} %param.12) | copy-start | bytes 1540
  90.5 1.0 copy-start.7
  90.6 1.0 copy-start.29
  90.6 1.0 copy-start.27
  92.0 15.5 %slice-start = ((s8[5505024]{0:T(1024)(128)(4,1)}), s8[1310720]{0:T(1024)(128)(4,1)S(1)}, s32[]{:S(2)}) async-start(s8[5505024]{0:T(1024)(128)(4,1)} %bitcast.125), calls=%async_computation.5 | async-start | bytes 2621440
  92.2 15.3 %slice-start.1 = ((s8[5505024]{0:T(1024)(128)(4,1)}), s8[4194304]{0:T(1024)(128)(4,1)S(1)}, s32[]{:S(2)}) async-start(s8[5505024]{0:T(1024)(128)(4,1)} %bitcast.125), calls=%async_computation.6 | async-start | bytes 8388608
  99.6 3.9 copy-start.19
  100.7 25.0 %collective-permute-start.1 = (bf16[2,512,512]{2,1,0:T(8,128)(2,1)}, bf16[2,512,512]{2,1,0:T(8,128)(2,1)}, u32[]{:S(2)}, u32[]{:S(2)}) collective-permute-start(bf16[2,512,512]{2,1,0:T(8,128)(2,1)} %pad_maximum_fusion.1), channel_id=1, source_target_pairs={{0,2},{2,4},{4,6},{6,8},{8,10},{10,12},{12,14},{14,16},{16,18},{18... | collective-permute-start | bytes 3145736 | tf_op jit(solution)/shard_map/ppermute | solution.py:18
  103.4 26.5 %collective-permute-start = (bf16[2,512,512]{2,1,0:T(8,128)(2,1)}, bf16[2,512,512]{2,1,0:T(8,128)(2,1)}, u32[]{:S(2)}, u32[]{:S(2)}) collective-permute-start(bf16[2,512,512]{2,1,0:T(8,128)(2,1)} %pad_maximum_fusion.1), channel_id=1, source_target_pairs={{0,4},{2,6},{4,8},{6,10},{8,12},{10,14},{12,16},{14,18},{16,20},{1... | collective-permute-start | bytes 3145736 | tf_op jit(solution)/shard_map/ppermute | solution.py:18
  121.1 1.7 copy-start.12
  121.1 1.7 copy-start.15
  123.9 6.0 copy-start.20
  158.2 10.8 %copy-start.26 = (bf16[512,4,2,128]{0,3,2,1:T(8,128)(2,1)S(1)}, bf16[512,4,2,128]{0,3,2,1:T(8,128)(2,1)}, u32[]{:S(2)}) copy-start(bf16[512,4,2,128]{0,3,2,1:T(8,128)(2,1)} %copy.103) | copy-start | bytes 3145732
  169.0 13.4 %copy-start.21 = (bf16[1536,4,128]{2,1,0:T(4,128)(2,1)S(1)}, bf16[1536,4,128]{2,1,0:T(4,128)(2,1)}, u32[]{:S(2)}) copy-start(bf16[1536,4,128]{2,1,0:T(4,128)(2,1)} %reshape_squeeze.15) | copy-start | bytes 4718596
  222.7 9.3 %copy-start.5 = (f32[4,1536,128,1]{1,2,3,0:T(8,128)S(1)}, f32[4,1536,128,1]{1,2,3,0:T(8,128)}, u32[]{:S(2)}) copy-start(f32[4,1536,128,1]{1,2,3,0:T(8,128)} %fusion.27) | copy-start | bytes 9437188
  232.0 3.0 copy-start
  232.0 5.6 copy-start.4
  235.0 29.3 %collective-permute-start.2 = (f32[2,512,512]{1,2,0:T(8,128)}, f32[2,512,512]{1,2,0:T(8,128)}, u32[]{:S(2)}, u32[]{:S(2)}) collective-permute-start(f32[2,512,512]{1,2,0:T(8,128)} %get-tuple-element.78), channel_id=1, source_target_pairs={{2,0},{4,2},{6,4},{8,6},{10,8},{12,10},{14,12},{16,14},{18,16},{20... | collective-permute-start | bytes 6291464 | tf_op jit(solution)/shard_map/ppermute | solution.py:18
  236.3 80.3 %collective-permute-start.3 = (f32[2,512,512]{1,2,0:T(8,128)}, f32[2,512,512]{1,2,0:T(8,128)}, u32[]{:S(2)}, u32[]{:S(2)}) collective-permute-start(f32[2,512,512]{1,2,0:T(8,128)} %get-tuple-element.79), channel_id=1, source_target_pairs={{4,0},{6,2},{8,4},{10,6},{12,8},{14,10},{16,12},{18,14},{20,16},{2... | collective-permute-start | bytes 6291464 | tf_op jit(solution)/shard_map/ppermute | solution.py:18
  245.6 6.5 copy-start.13
  245.6 6.5 copy-start.16
  252.1 4.7 copy-start.33
  254.8 1.4 copy-start.2
  254.8 2.0 copy-start.3
  256.8 1.5 copy-start.18
  258.3 58.3 %copy-start.1 = (f32[4,128,1536,1]{2,1,3,0:T(8,128)S(1)}, f32[4,128,1536,1]{2,1,3,0:T(8,128)}, u32[]{:S(2)}) copy-start(f32[4,128,1536,1]{2,1,3,0:T(8,128)} %copy-done) | copy-start | bytes 9437188
  258.3 58.3 %copy-start.6 = (f32[4,1536,128,1]{1,2,3,0:T(8,128)S(1)}, f32[4,1536,128,1]{1,2,3,0:T(8,128)}, u32[]{:S(2)}) copy-start(f32[4,1536,128,1]{1,2,3,0:T(8,128)} %fusion.27) | copy-start | bytes 9437188
  262.9 1.3 copy-start.17
  319.5 4.0 copy-start.23
  319.6 5.4 copy-start.8
  319.6 5.4 copy-start.32
  321.5 3.7 copy-start.30
  321.5 3.7 copy-start.28
  375.4 14.1 %copy-start.10 = (bf16[512,4,128]{0,2,1:T(8,128)(2,1)S(1)}, bf16[512,4,128]{0,2,1:T(8,128)(2,1)}, u32[]{:S(2)}) copy-start(bf16[512,4,128]{0,2,1:T(8,128)(2,1)} %fusion.21) | copy-start | bytes 1572868
  375.4 290.0 %reduce-scatter.5.cloned.1.call-start = ((), (), s32[]{:S(2)}) async-start(), calls=%async_computation.3 | async-start | bytes 8257536 | tf_op jit(solution)/shard_map/reduce_scatter | solution.py:216
  416.4 1.5 copy-start.25
Sparse Core Ops, SparseCore 0:
  9.5 74.2 all-gather.1
  375.5 219.3 reduce-scatter.6
  597.8 67.6 reduce-scatter.4
where the time goes:
time: 679 us; the launch traced here: 672 us
  waiting for transfers between devices  367 us (54%)
  matrix products  155 us (23%)
  local copies, waits for them, and re-layouts  82.5 us (12%)
  other arithmetic  43.8 us (6%)
  between operations  14.6 us (2%)
  starting transfers between devices  9.46 us (1%)
    unnamed x4, waiting for transfers between devices  176 us
    all_gather x1, waiting for transfers between devices, per_device(): gathered = lax.all_gather(hidden, 'heads', axis=0, tiled=True)  69.4 us
    reduce_scatter x1, waiting for transfers between devices, per_device(): lax.psum_scatter((partial_sum + lax.dot_general(grad_value, value_weight,...  64.7 us
    ppermute x4, waiting for transfers between devices, passed_along(): return lax.ppermute(block, axis, route)  56.5 us
    unnamed x83, local copies, waits for them, and re-layouts  53.7 us
    dot_general x1, matrix products, per_device(): lax.dot_general(gathered, jnp.concatenate([grad_query, grad_key, grad_val...  19 us
    dot_general x1, matrix products, attend_backward(): jnp.einsum('qkgd,jkd->kgqj', grad_grid, value_grid, preferred_element_typ...  16.1 us
    dot_general x1, matrix products, per_device(): lax.dot_general(grad_value, value_weight, back_contract, preferred_elemen...  15.1 us
  transfers between devices with their start and end apart: 7, of which 5 were waited for; matrix products, arithmetic and copies ran while one was open for 14% of the time, Pallas kernels for 0%

commit v1 on v0

v1 whole, which is shorter than its diff:
```python
import functools
import math

import jax
import jax.numpy as jnp
from jax import lax
from jax.experimental import pallas as pl
from jax.experimental.pallas import tpu as pltpu
from jax.sharding import PartitionSpec as P

HEAD_DIM = 128
WINDOW = 1024
SCALAR = 168
HEADS = 16
KV_HEADS = 8
GROUP = HEADS // KV_HEADS
TILE = 256
LOW = -1e30
F32 = jnp.float32
BF16 = jnp.bfloat16
VMEM_LIMIT = 48 * 1024 * 1024


def passed_along(block, axis, distance):
    devices = range(lax.axis_size(axis))
    route = [(i - distance, i) for i in devices if i - distance in devices]
    return lax.ppermute(block, axis, route)


def rotated(block, axis, distance):
    size = lax.axis_size(axis)
    return lax.ppermute(block, axis, [(i, (i + distance) % size) for i in range(size)])


def rope_tables(positions):
    half_size = HEAD_DIM // 2
    indices = jnp.arange(half_size, dtype=F32)
    inverse = jnp.exp(indices * (-2.0 * math.log(10000.0) / HEAD_DIM))
    angles = positions.astype(F32)[:, None] * inverse[None, :]
    cosine, sine = jnp.cos(angles), jnp.sin(angles)
    return (
        jnp.concatenate([cosine, cosine], axis=1),
        jnp.concatenate([-sine, sine], axis=1),
    )


def head_map(u, cosine, sine, gain, factor):
    scale = lax.rsqrt(jnp.mean(u * u, axis=-1, keepdims=True) + 1e-06)
    normed = u * scale * gain
    turned = normed * cosine + pltpu.roll(normed, HEAD_DIM // 2, 1) * sine
    return turned * factor


def head_map_back(u, cosine, sine, gain, factor, cot):
    scale = lax.rsqrt(jnp.mean(u * u, axis=-1, keepdims=True) + 1e-06)
    cot = cot * factor
    inner = (cot * cosine + pltpu.roll(cot * sine, HEAD_DIM // 2, 1)) * gain
    mean = jnp.mean(inner * u, axis=-1, keepdims=True)
    return scale * inner - u * (scale * scale * scale * mean)


def key_kernel(key_ref, value_ref, cos_ref, sin_ref, gain_ref, pair_ref):
    pair_ref[0] = head_map(key_ref[...], cos_ref[...], sin_ref[...], gain_ref[...], 1.0).astype(BF16)
    pair_ref[1] = value_ref[...].astype(BF16)


def key_grad_kernel(reach, key_ref, cos_ref, sin_ref, gain_ref, own_ref, *rest):
    received, (key_out, value_out) = rest[:reach], rest[reach:]
    key_cot, value_cot = own_ref[0], own_ref[1]
    for ref in received:
        key_cot += ref[0].astype(F32)
        value_cot += ref[1].astype(F32)
    key_out[...] = head_map_back(
        key_ref[...], cos_ref[...], sin_ref[...], gain_ref[...], 1.0, key_cot
    ).astype(BF16)
    value_out[...] = value_cot.astype(BF16)


def dot_nt(a, b):
    return lax.dot_general(a, b, (((1,), (1,)), ((), ())), preferred_element_type=F32)


def dot_nn(a, b):
    return jnp.dot(a, b, preferred_element_type=F32)


def attention_kernel(
    rows, base_ref, query_ref, out_grad_ref, span_ref, cos_ref, sin_ref, gain_ref,
    attention_ref, query_grad_ref, own_ref, far_ref, total,
):
    chunks = WINDOW // TILE + 1
    factor = SCALAR ** (-0.5)
    base = base_ref[0]
    total[...] = jnp.zeros_like(total)
    key_turned = span_ref[0].T
    value_turned = span_ref[1].T
    row = lax.broadcasted_iota(jnp.int32, (TILE, TILE), 0)
    column = lax.broadcasted_iota(jnp.int32, (TILE, TILE), 1)
    for part in range(rows // TILE):
        at = slice(part * TILE, (part + 1) * TILE)
        keys = [slice((part + c) * TILE, (part + c + 1) * TILE) for c in range(chunks)]
        shift = [
            jnp.where(base - WINDOW + (part + c) * TILE >= 0, 0.0, LOW).astype(F32)
            for c in range(chunks)
        ]
        for head in range(GROUP):
            lanes = slice(head * HEAD_DIM, (head + 1) * HEAD_DIM)
            proj = query_ref[at, lanes]
            query = head_map(proj, cos_ref[at], sin_ref[at], gain_ref[...], factor).astype(BF16)
            out_grad = out_grad_ref[at, lanes]
            scores = [dot_nt(span_ref[0, key], query) for key in keys]
            scores[0] = jnp.where(row > column, scores[0], LOW)
            scores[-1] = jnp.where(row <= column, scores[-1], LOW)
            highest = jnp.full((1, TILE), LOW, F32)
            for s, b in zip(scores, shift):
                highest = jnp.maximum(highest, jnp.max(s, axis=0, keepdims=True) + b)
            weights = [jnp.exp(s - (highest - b)) for s, b in zip(scores, shift)]
            sums = jnp.sum(weights[0], axis=0, keepdims=True)
            for w in weights[1:]:
                sums += jnp.sum(w, axis=0, keepdims=True)
            inverse = 1.0 / sums
            weights = [w * inverse for w in weights]
            low = [w.astype(BF16) for w in weights]
            output = dot_nn(value_turned[:, keys[0]], low[0])
            for key, w in zip(keys[1:], low[1:]):
                output += dot_nn(value_turned[:, key], w)
            output = output.astype(BF16)
            attention_ref[at, lanes] = output.T
            delta = jnp.sum(
                out_grad.T.astype(F32) * output.astype(F32), axis=0, keepdims=True
            )
            query_cot = jnp.zeros((HEAD_DIM, TILE), F32)
            for key, w, wl in zip(keys, weights, low):
                products = dot_nt(span_ref[1, key], out_grad)
                moves = (w * (products - delta)).astype(BF16)
                query_cot += dot_nn(key_turned[:, key], moves)
                total[0, key] += dot_nn(moves, query)
                total[1, key] += dot_nn(wl, out_grad)
            query_grad_ref[at, lanes] = head_map_back(
                proj, cos_ref[at], sin_ref[at], gain_ref[...], factor, query_cot.T
            ).astype(BF16)
    far_ref[...] = total[:, :WINDOW].astype(BF16)
    own_ref[...] = total[:, WINDOW:]


def params():
    return pltpu.CompilerParams(vmem_limit_bytes=VMEM_LIMIT)


def whole(shape):
    return pl.BlockSpec(shape, lambda h: (0,) * len(shape))


def per_head(rows, width=HEAD_DIM):
    return pl.BlockSpec((rows, width), lambda h: (0, h))


def pair_head(rows):
    return pl.BlockSpec((2, rows, HEAD_DIM), lambda h: (0, 0, h))


def per_device(hidden, query_weight, key_weight, value_weight, query_gain, key_gain, out_grad):
    rows = out_grad.shape[0]
    share, depth = hidden.shape
    peers = lax.axis_size("heads")
    me = lax.axis_index("heads")
    reach = WINDOW // rows
    base = lax.axis_index("ctx") * rows
    query_width, key_width = query_weight.shape[1], key_weight.shape[1]
    kv_heads = key_width // HEAD_DIM

    pieces = 3
    step = depth // pieces
    gathered, query_proj, key_proj, value_proj = [], None, None, None
    for piece in range(pieces):
        span = slice(piece * step, (piece + 1) * step)
        mine = hidden[:, span]
        block = jnp.zeros((rows, step), BF16)
        block = lax.dynamic_update_slice(block, mine, (me * share, 0))
        for distance in range(1, peers):
            other = rotated(mine, "heads", distance)
            block = lax.dynamic_update_slice(
                block, other, (lax.rem(me + peers - distance, peers) * share, 0)
            )
        gathered.append(block)
        q = dot_nn(block, query_weight[span])
        k = dot_nn(block, key_weight[span])
        v = dot_nn(block, value_weight[span])
        query_proj = q if query_proj is None else query_proj + q
        key_proj = k if key_proj is None else key_proj + k
        value_proj = v if value_proj is None else value_proj + v

    cosine, sine = rope_tables(base + jnp.arange(rows, dtype=jnp.int32))
    query_gain, key_gain = query_gain[None, :], key_gain[None, :]
    table = whole((rows, HEAD_DIM))
    gain = whole((1, HEAD_DIM))
    pair = pl.pallas_call(
        key_kernel,
        grid=(kv_heads,),
        in_specs=[per_head(rows), per_head(rows), table, table, gain],
        out_specs=pair_head(rows),
        out_shape=jax.ShapeDtypeStruct((2, rows, key_width), BF16),
        compiler_params=params(),
    )(key_proj, value_proj, cosine, sine, key_gain)
    received = [passed_along(pair, "ctx", distance) for distance in range(1, reach + 1)]
    span = jnp.concatenate(received[::-1] + [pair], axis=1)

    attention, grad_query, own, far = pl.pallas_call(
        functools.partial(attention_kernel, rows),
        grid=(kv_heads,),
        in_specs=[
            pl.BlockSpec(memory_space=pltpu.SMEM),
            per_head(rows, GROUP * HEAD_DIM),
            per_head(rows, GROUP * HEAD_DIM),
            pair_head(rows + WINDOW),
            table,
            table,
            gain,
        ],
        out_specs=[
            per_head(rows, GROUP * HEAD_DIM),
            per_head(rows, GROUP * HEAD_DIM),
            pair_head(rows),
            pair_head(WINDOW),
        ],
        out_shape=[
            jax.ShapeDtypeStruct((rows, query_width), BF16),
            jax.ShapeDtypeStruct((rows, query_width), BF16),
            jax.ShapeDtypeStruct((2, rows, key_width), F32),
            jax.ShapeDtypeStruct((2, WINDOW, key_width), BF16),
        ],
        scratch_shapes=[pltpu.VMEM((2, rows + WINDOW, HEAD_DIM), F32)],
        compiler_params=params(),
    )(base[None], query_proj, out_grad, span, cosine, sine, query_gain)

    tokens = jnp.concatenate(gathered, axis=1)
    grad_scale = float(lax.axis_size("ctx") * rows) ** (-0.5)

    def weight_grad(columns):
        partial = (
            lax.dot_general(
                tokens, columns, (((0,), (0,)), ((), ())), preferred_element_type=F32
            )
            * grad_scale
        ).astype(BF16)
        return lax.psum_scatter(partial, "ctx", scatter_dimension=0, tiled=True).astype(F32)

    query_weight_grad = weight_grad(grad_query)
    backs = [
        passed_along(far[:, (reach - distance) * rows : (reach - distance + 1) * rows], "ctx", -distance)
        for distance in range(1, reach + 1)
    ]
    grad_key, grad_value = pl.pallas_call(
        functools.partial(key_grad_kernel, reach),
        grid=(kv_heads,),
        in_specs=[per_head(rows), table, table, gain] + [pair_head(rows)] * (1 + reach),
        out_specs=[per_head(rows), per_head(rows)],
        out_shape=[jax.ShapeDtypeStruct((rows, key_width), BF16)] * 2,
        compiler_params=params(),
    )(key_proj, cosine, sine, key_gain, own, *backs)

    def input_term(owner):
        def cut(array):
            return lax.dynamic_slice_in_dim(array, owner * share, share, 0)

        return (
            dot_nt(cut(grad_query), query_weight)
            + dot_nt(cut(grad_key), key_weight)
            + dot_nt(cut(grad_value), value_weight)
        ).astype(BF16)

    arrived = [
        rotated(input_term(lax.rem(me + distance, peers)), "heads", distance)
        for distance in range(1, peers)
    ]
    pair_weight_grad = weight_grad(jnp.concatenate([grad_key, grad_value], axis=1))
    input_sum = input_term(me).astype(F32)
    for term in arrived:
        input_sum += term.astype(F32)
    return (
        attention,
        input_sum.astype(BF16),
        query_weight_grad,
        pair_weight_grad[:, :key_width],
        pair_weight_grad[:, key_width:],
    )


def solution(mesh):
    return jax.shard_map(
        per_device,
        mesh=mesh,
        in_specs=(
            P(("ctx", "heads"), None),
            P(None, "heads"),
            P(None, "heads"),
            P(None, "heads"),
            P(),
            P(),
            P("ctx", "heads"),
        ),
        out_specs=(
            P("ctx", "heads"),
            P(("ctx", "heads"), None),
            P("ctx", "heads"),
            P("ctx", "heads"),
            P("ctx", "heads"),
        ),
        check_vma=False,
    )
```

time: 679 us -> 436 us (0.64)
  waiting for transfers between devices: 367 us -> 249 us
  local copies, waits for them, and re-layouts: 82.5 us -> 20 us
  matrix products: 155 us -> 94.2 us
  other arithmetic: 43.8 us -> 5.28 us
  Pallas kernels: 0 us -> 37.7 us
    unnamed x4 -> x2, waiting for transfers between devices: 176 us -> 0.03 us
    all_gather x1 -> x0, waiting for transfers between devices: 69.4 us -> none  [per_device(): gathered = lax.all_gather(hidden, 'heads', axis=0, tiled=True)]
    ppermute x0 -> x4, waiting for transfers between devices: none -> 67 us  [rotated(): lax.ppermute(block, axis, [(i, (i + distance) % size) for i in range(size)])]
    dot_general x13 -> x17, matrix products: 155 us -> 94.2 us  [the longest x6 40.3 us: dot_nt(): lax.dot_general(a, b, (((1,), (1,)), ((), ())), preferred_element_type=F32)]
    reduce_scatter x1 -> x2, waiting for transfers between devices: 64.7 us -> 121 us  [weight_grad(): lax.psum_scatter(partial, 'ctx', scatter_dimension=0, tiled=True)]
    unnamed x83 -> x24, local copies, waits for them, and re-layouts: 53.7 us -> 2.57 us
    pallas_call x0 -> x3, Pallas kernels: none -> 37.7 us  [the longest x1 32.7 us: per_device(): pl.pallas_call(functools.partial(attention_kernel, rows), grid=(kv_heads,...]
    reduce_sum x4 -> x0, other arithmetic: 13.5 us -> none  [the longest x1 10.8 us: attend_forward(): total = jnp.sum(jnp.exp(masked - highest), axis=-1, keepdims=True)]
  transfers between devices with their start and end apart: 7 -> 10, of which waited for: 5 -> 8; matrix products, arithmetic and copies ran while one was open for 14% -> 20% of each run, Pallas kernels for 0% -> 1%
where the time goes in v1:
time: 436 us; the launch traced here: 435 us
  waiting for transfers between devices  249 us (57%)
  matrix products  94.2 us (22%)
  Pallas kernels  37.7 us (9%)
  local copies, waits for them, and re-layouts  20 us (5%)
  between operations  14.3 us (3%)
  starting transfers between devices  14.2 us (3%)
  other arithmetic  5.28 us (1%)
    reduce_scatter x2, waiting for transfers between devices, weight_grad(): lax.psum_scatter(partial, 'ctx', scatter_dimension=0, tiled=True)  121 us
    ppermute x4, waiting for transfers between devices, rotated(): lax.ppermute(block, axis, [(i, (i + distance) % size) for i in range(size)])  67 us
    ppermute x4, waiting for transfers between devices, passed_along(): return lax.ppermute(block, axis, route)  60.8 us
    dot_general x6, matrix products, dot_nt(): lax.dot_general(a, b, (((1,), (1,)), ((), ())), preferred_element_type=F32)  40.3 us
    pallas_call x1, Pallas kernels, per_device(): pl.pallas_call(functools.partial(attention_kernel, rows), grid=(kv_heads,...  32.7 us
    dot_general x9, matrix products, dot_nn(): return jnp.dot(a, b, preferred_element_type=F32)  30.8 us
    dot_general x2, matrix products, weight_grad(): lax.dot_general(tokens, columns, (((0,), (0,)), ((), ())), preferred_elem...  23.1 us
  transfers between devices with their start and end apart: 10, of which 8 were waited for; matrix products, arithmetic and copies ran while one was open for 20% of the time, Pallas kernels for 1%

profile of v1, /device:TPU:0, one launch (start us, length us, event | category | flops | bytes accessed | tf_op | source)
XLA Modules:
  0.0 434.8 jit_solution(10113513789382490270)
XLA Ops:
  7.2 0.0 reduce-scatter.3.cloned.1.call-start
  7.2 1.4 broadcast.16.clone
  8.6 3.8 fusion.55
  12.5 3.0 collective-permute-start.2
  15.4 0.0 collective-permute-start.1
  15.5 2.0 collective-permute-start
  17.5 1.3 broadcast.16.clone.2
  18.8 1.0 constant_dynamic-update-slice_fusion.1
  19.8 0.1 broadcast.16.clone.1
  19.9 0.1 constant_dynamic-update-slice_fusion.3
  20.0 1.0 fusion.46
  21.0 0.2 pad_maximum_fusion.4
  21.2 15.7 %collective-permute-done.2 = bf16[256,1792]{1,0:T(8,128)(2,1)} collective-permute-done((bf16[256,1792]{1,0:T(8,128)(2,1)}, bf16[256,1792]{1,0:T(8,128)(2,1)}, u32[]{:S(2)}, u32[]{:S(2)}) %collective-permute-start.2) | collective-permute-done | bytes 917536 | tf_op jit(solution)/shard_map/ppermute | solution.py:32
  36.9 2.2 constant_dynamic-update-slice_fusion
  39.1 3.3 fusion.11
  42.4 0.0 slice-start.1
  42.4 14.2 %collective-permute-done.1 = bf16[256,1792]{1,0:T(8,128)(2,1)} collective-permute-done((bf16[256,1792]{1,0:T(8,128)(2,1)}, bf16[256,1792]{1,0:T(8,128)(2,1)}, u32[]{:S(2)}, u32[]{:S(2)}) %collective-permute-start.1) | collective-permute-done | bytes 917536 | tf_op jit(solution)/shard_map/ppermute | solution.py:32
  56.6 1.3 constant_dynamic-update-slice_fusion.2
  57.9 0.0 copy-start.7
  57.9 3.3 fusion.13
  61.2 2.6 fusion.17
  63.8 1.1 fusion.19
  64.9 10.5 %collective-permute-done = bf16[256,1792]{1,0:T(8,128)(2,1)} collective-permute-done((bf16[256,1792]{1,0:T(8,128)(2,1)}, bf16[256,1792]{1,0:T(8,128)(2,1)}, u32[]{:S(2)}, u32[]{:S(2)}) %collective-permute-start) | collective-permute-done | bytes 917536 | tf_op jit(solution)/shard_map/ppermute | solution.py:32
  75.4 2.2 constant_dynamic-update-slice_fusion.4
  77.7 3.2 fusion.32.value_ref
  80.8 0.0 copy-start.2
  80.9 2.6 fusion.26.key_ref
  83.5 0.0 copy-done.2
  83.5 1.4 shard_map.110
  84.9 3.7 collective-permute-start.3
  88.6 1.4 collective-permute-start.4
  90.0 4.1 fusion.7
  94.1 4.7 %fusion.9 = f32[512,1024]{1,0:T(8,128)S(1)} fusion(bf16[512,1792]{1,0:T(8,128)(2,1)} %constant_dynamic-update-slice_fusion.4, bf16[5376,1024]{1,0:T(8,128)(2,1)} %param.8), kind=kOutput, calls=%fused_computation.16 | convolution fusion | flops 1879048192 | bytes 7602176 | tf_op jit(solution)/shard_map/dot_general | solution.py:84
  98.7 6.0 %add_add_fusion.query_ref = f32[512,1024]{1,0:T(8,128)} fusion(f32[512,1024]{1,0:T(8,128)S(1)} %fusion.9, f32[512,1024]{1,0:T(8,128)S(1)} %fusion.7, bf16[512,1792]{1,0:T(8,128)(2,1)} %constant_dynamic-update-slice_fusion, bf16[5376,1024]{1,0:T(8,128)(2,1)} %param.8), kind=kOutput, calls=%fused_computation.19 | convolution fusion | flops 1880096768 | bytes 11796480 | tf_op jit(solution)/shard_map/dot_general | solution.py:84
  104.7 7.4 %collective-permute-done.3 = bf16[2,512,512]{2,1,0:T(8,128)(2,1)S(1)} collective-permute-done((bf16[2,512,512]{2,1,0:T(8,128)(2,1)S(1)}, bf16[2,512,512]{2,1,0:T(8,128)(2,1)S(1)}, u32[]{:S(2)}, u32[]{:S(2)}) %collective-permute-start.3) | collective-permute-done | bytes 1048608 | tf_op jit(solution)/shard_map/ppermute | solution.py:27
  112.1 0.0 collective-permute-done.4
  112.1 1.7 pad_maximum_fusion.1.span_ref
  113.9 32.7 %shard_map.111 = (bf16[512,1024]{1,0:T(8,128)(2,1)}, bf16[512,1024]{1,0:T(8,128)(2,1)S(1)}, f32[2,512,512]{2,1,0:T(8,128)S(1)}, bf16[2,1024,512]{2,1,0:T(8,128)(2,1)}) custom-call(s32[1]{0:T(128)} %bitcast.base_ref, f32[512,1024]{1,0:T(8,128)} %add_add_fusion.query_ref, bf16[512,1024]{1,0:T(8,128)(2,1)S(1)} %copy-done.1, ...), custom_call_target="tpu_custom_call" | custom-call | tf_op jit(solution)/shard_map/pallas_call | solution.py:208
  146.6 1.3 copy-done
  147.9 11.7 %multiply_convert_fusion.1 = bf16[5376,1024]{1,0:T(8,128)(2,1)} fusion(bf16[512,1024]{1,0:T(8,128)(2,1)S(1)} %get-tuple-element.12, bf16[512,1792]{1,0:T(8,128)(2,1)} %constant_dynamic-update-slice_fusion, bf16[512,1792]{1,0:T(8,128)(2,1)} %copy-done.7, bf16[512,1792]{1,0:T(8,128)(2,1)} %constant_dynamic-update-slice_fusion.4), kind=kOutput, calls=%fused_computation.1 | convolution fusion | flops 5664669696 | bytes 17563648 | tf_op jit(solution)/shard_map/dot_general | solution.py:241
  159.6 0.0 copy-done.4
  159.6 0.0 reduce-scatter.3.cloned.1.call-update
  159.6 0.0 reduce-scatter.5.cloned.1.call-start
  159.7 1.7 fusion.56
  161.4 1.3 collective-permute-start.5
  162.7 1.3 collective-permute-start.6
  164.0 10.7 %collective-permute-done.5.rest_0_ = bf16[2,512,512]{2,1,0:T(8,128)(2,1)S(1)} collective-permute-done((bf16[2,512,512]{2,1,0:T(8,128)(2,1)S(1)}, bf16[2,512,512]{2,1,0:T(8,128)(2,1)S(1)}, u32[]{:S(2)}, u32[]{:S(2)}) %collective-permute-start.5) | collective-permute-done | bytes 1048608 | tf_op jit(solution)/shard_map/ppermute | solution.py:27
  174.7 42.7 %collective-permute-done.6.rest_1_ = bf16[2,512,512]{2,1,0:T(8,128)(2,1)S(1)} collective-permute-done((bf16[2,512,512]{2,1,0:T(8,128)(2,1)S(1)}, bf16[2,512,512]{2,1,0:T(8,128)(2,1)S(1)}, u32[]{:S(2)}, u32[]{:S(2)}) %collective-permute-start.6) | collective-permute-done | bytes 1048608 | tf_op jit(solution)/shard_map/ppermute | solution.py:27
  217.4 3.6 shard_map.112
  221.0 11.4 %multiply_convert_fusion = bf16[5376,1024]{1,0:T(8,128)(2,1)} fusion(bf16[512,1792]{1,0:T(8,128)(2,1)} %constant_dynamic-update-slice_fusion, bf16[512,1792]{1,0:T(8,128)(2,1)} %copy-done.7, bf16[512,1792]{1,0:T(8,128)(2,1)} %constant_dynamic-update-slice_fusion.4, bf16[512,512]{1,0:T(8,128)(2,1)S(1)} %get-tuple-element.16, ...), kind=kOutput, calls=%fused_computation | convolution fusion | flops 5666766848 | bytes 17563648 | tf_op jit(solution)/shard_map/dot_general | solution.py:241
  232.3 0.0 reduce-scatter.5.cloned.1.call-update
  232.4 1.2 copy-done.5
  233.6 6.0 %fusion.38 = f32[256,5376]{1,0:T(8,128)S(1)} fusion(bf16[5376,1024]{1,0:T(8,128)(2,1)} %param.8, bf16[512,1024]{1,0:T(8,128)(2,1)S(1)} %copy-done.5, s32[]{:T(128)S(6)} %select_n.5), kind=kOutput, calls=%fused_computation.39 | convolution fusion | flops 2818572288 | bytes 17039364 | tf_op jit(solution)/shard_map/dot_general | solution.py:80
  239.6 4.5 %convolution_add_fusion.1 = f32[256,5376]{1,0:T(8,128)S(1)} fusion(f32[256,5376]{1,0:T(8,128)S(1)} %fusion.38, bf16[5376,512]{1,0:T(8,128)(2,1)} %param.9, bf16[512,512]{1,0:T(8,128)(2,1)S(1)} %get-tuple-element.15, s32[]{:T(128)S(6)} %select_n.5), kind=kOutput, calls=%fused_computation.3 | convolution fusion | flops 1410662400 | bytes 16777220 | tf_op jit(solution)/shard_map/dot_general | solution.py:80
  244.1 0.0 slice-start.2
  244.1 6.1 %fusion.4 = bf16[256,5376]{1,0:T(8,128)(2,1)} fusion(f32[256,5376]{1,0:T(8,128)S(1)} %convolution_add_fusion.1, bf16[5376,512]{1,0:T(8,128)(2,1)} %param.10, bf16[512,512]{1,0:T(8,128)(2,1)S(1)} %get-tuple-element.16, s32[]{:T(128)S(6)} %select_n.5), kind=kOutput, calls=%fused_computation.10 | convolution fusion | flops 1412038656 | bytes 14024708 | tf_op jit(solution)/shard_map/dot_general | solution.py:80
  250.2 1.5 collective-permute-start.7
  251.7 13.3 %fusion.40 = f32[256,5376]{1,0:T(8,128)} fusion(bf16[5376,1024]{1,0:T(8,128)(2,1)} %param.8, bf16[512,1024]{1,0:T(8,128)(2,1)S(1)} %copy-done.5, s32[]{:T(128)S(6)} %select_n.4), kind=kOutput, calls=%fused_computation.41 | convolution fusion | flops 2818572288 | bytes 17039364 | tf_op jit(solution)/shard_map/dot_general | solution.py:80
  264.9 4.4 %convolution_add_fusion.3 = f32[256,5376]{1,0:T(8,128)S(1)} fusion(f32[256,5376]{1,0:T(8,128)} %fusion.40, bf16[5376,512]{1,0:T(8,128)(2,1)S(1)} %bitcast.25, bf16[512,512]{1,0:T(8,128)(2,1)S(1)} %get-tuple-element.15, s32[]{:T(128)S(6)} %select_n.4), kind=kOutput, calls=%fused_computation.5 | convolution fusion | flops 1410662400 | bytes 16777220 | tf_op jit(solution)/shard_map/dot_general | solution.py:80
  269.3 26.6 %collective-permute-done.7 = bf16[256,5376]{1,0:T(8,128)(2,1)S(1)} collective-permute-done((bf16[256,5376]{1,0:T(8,128)(2,1)}, bf16[256,5376]{1,0:T(8,128)(2,1)S(1)}, u32[]{:S(2)}, u32[]{:S(2)}) %collective-permute-start.7) | collective-permute-done | bytes 2752544 | tf_op jit(solution)/shard_map/ppermute | solution.py:32
  295.9 6.0 %fusion.3 = bf16[256,5376]{1,0:T(8,128)(2,1)} fusion(f32[256,5376]{1,0:T(8,128)S(1)} %convolution_add_fusion.3, bf16[5376,512]{1,0:T(8,128)(2,1)} %param.10, bf16[256,5376]{1,0:T(8,128)(2,1)S(1)} %collective-permute-done.7, bf16[512,512]{1,0:T(8,128)(2,1)S(1)} %get-tuple-element.16, s32[]{:T(128)S(6)} %select_n.4), kind=kOutput, calls=%fused_computation.9 | convolution fusion | flops 1417543680 | bytes 16777220 | tf_op jit(solution)/shard_map/dot_general | solution.py:80
  302.0 2.3 convert_element_type.41
  304.3 121.3 %reduce-scatter.5.cloned.1.call-done = bf16[336,1024]{1,0:T(8,128)(2,1)} async-done(((bf16[5376,1024]{1,0:T(8,128)(2,1)}), bf16[336,1024]{1,0:T(8,128)(2,1)}) %reduce-scatter.5.cloned.1.call-update) | async-done | bytes 688144 | tf_op jit(solution)/shard_map/reduce_scatter | solution.py:246
  425.6 2.3 fusion.57
  (21 shorter events, 0.0 us)
Async XLA Ops:
  7.2 294.8 %reduce-scatter.3.cloned.1.call-start = ((), (), s32[]{:S(2)}) async-start(), calls=%async_computation.2 | async-start | bytes 11698176 | tf_op jit(solution)/shard_map/reduce_scatter | solution.py:246
  8.6 10.2 %copy-start.6 = (bf16[256,5376]{1,0:T(8,128)(2,1)S(1)}, bf16[256,5376]{1,0:T(8,128)(2,1)}, u32[]{:S(2)}) copy-start(bf16[256,5376]{1,0:T(8,128)(2,1)} %param.7) | copy-start | bytes 8257540
  12.5 24.5 %collective-permute-start.2 = (bf16[256,1792]{1,0:T(8,128)(2,1)}, bf16[256,1792]{1,0:T(8,128)(2,1)}, u32[]{:S(2)}, u32[]{:S(2)}) collective-permute-start(bf16[256,1792]{1,0:T(8,128)(2,1)} %get-tuple-element.20), channel_id=1, source_target_pairs={{0,1},{1,0},{2,3},{3,2},{4,5},{5,4},{6,7},{7,6},{8,9},{9,8},{10,11... | collective-permute-start | bytes 2752520 | tf_op jit(solution)/shard_map/ppermute | solution.py:32
  15.4 41.2 %collective-permute-start.1 = (bf16[256,1792]{1,0:T(8,128)(2,1)}, bf16[256,1792]{1,0:T(8,128)(2,1)}, u32[]{:S(2)}, u32[]{:S(2)}) collective-permute-start(bf16[256,1792]{1,0:T(8,128)(2,1)} %get-tuple-element.17), channel_id=1, source_target_pairs={{0,1},{1,0},{2,3},{3,2},{4,5},{5,4},{6,7},{7,6},{8,9},{9,8},{10,11... | collective-permute-start | bytes 2752520 | tf_op jit(solution)/shard_map/ppermute | solution.py:32
  15.5 60.0 %collective-permute-start = (bf16[256,1792]{1,0:T(8,128)(2,1)}, bf16[256,1792]{1,0:T(8,128)(2,1)}, u32[]{:S(2)}, u32[]{:S(2)}) collective-permute-start(bf16[256,1792]{1,0:T(8,128)(2,1)} %get-tuple-element.19), channel_id=1, source_target_pairs={{0,1},{1,0},{2,3},{3,2},{4,5},{5,4},{6,7},{7,6},{8,9},{9,8},{10,11... | collective-permute-start | bytes 2752520 | tf_op jit(solution)/shard_map/ppermute | solution.py:32
  39.1 22.0 %slice-start = ((s8[5505024]{0:T(1024)(128)(4,1)}), s8[4194304]{0:T(1024)(128)(4,1)S(1)}, s32[]{:S(2)}) async-start(s8[5505024]{0:T(1024)(128)(4,1)} %bitcast.22), calls=%async_computation.4 | async-start | bytes 8388608
  42.4 18.7 %slice-start.1 = ((s8[5505024]{0:T(1024)(128)(4,1)}), s8[1310720]{0:T(1024)(128)(4,1)S(1)}, s32[]{:S(2)}) async-start(s8[5505024]{0:T(1024)(128)(4,1)} %bitcast.22), calls=%async_computation.5 | async-start | bytes 2621440
  57.9 32.1 %copy-start.7 = (bf16[512,1792]{1,0:T(8,128)(2,1)}, bf16[512,1792]{1,0:T(8,128)(2,1)S(1)}, u32[]{:S(2)}) copy-start(bf16[512,1792]{1,0:T(8,128)(2,1)S(1)} %constant_dynamic-update-slice_fusion.2) | copy-start | bytes 5505028
  80.8 2.6 copy-start.2
  84.9 27.2 %collective-permute-start.3 = (bf16[2,512,512]{2,1,0:T(8,128)(2,1)S(1)}, bf16[2,512,512]{2,1,0:T(8,128)(2,1)S(1)}, u32[]{:S(2)}, u32[]{:S(2)}) collective-permute-start(bf16[2,512,512]{2,1,0:T(8,128)(2,1)S(1)} %shard_map.110), channel_id=1, source_target_pairs={{0,4},{2,6},{4,8},{6,10},{8,12},{10,14},{12,16},{14,18},{16,20},{1... | collective-permute-start | bytes 3145736 | tf_op jit(solution)/shard_map/ppermute | solution.py:27
  88.6 23.5 %collective-permute-start.4 = (bf16[2,512,512]{2,1,0:T(8,128)(2,1)S(1)}, bf16[2,512,512]{2,1,0:T(8,128)(2,1)S(1)}, u32[]{:S(2)}, u32[]{:S(2)}) collective-permute-start(bf16[2,512,512]{2,1,0:T(8,128)(2,1)S(1)} %shard_map.110), channel_id=1, source_target_pairs={{0,2},{2,4},{4,6},{6,8},{8,10},{10,12},{12,14},{14,16},{16,18},{18... | collective-permute-start | bytes 3145736 | tf_op jit(solution)/shard_map/ppermute | solution.py:27
  104.7 9.2 %copy-start.1 = (bf16[512,1024]{1,0:T(8,128)(2,1)S(1)}, bf16[512,1024]{1,0:T(8,128)(2,1)}, u32[]{:S(2)}) copy-start(bf16[512,1024]{1,0:T(8,128)(2,1)} %out_grad_ref.1) | copy-start | bytes 3145732
  104.7 9.2 %copy-start.3 = (f32[128]{0:T(128)S(1)}, f32[128]{0:T(128)}, u32[]{:S(2)}) copy-start(f32[128]{0:T(128)} %param.11) | copy-start | bytes 1540
  146.6 1.3 copy-start
  147.9 11.7 %copy-start.4 = (bf16[512,1024]{1,0:T(8,128)(2,1)}, bf16[512,1024]{1,0:T(8,128)(2,1)S(1)}, u32[]{:S(2)}) copy-start(bf16[512,1024]{1,0:T(8,128)(2,1)S(1)} %get-tuple-element.12) | copy-start | bytes 3145732
  159.6 266.0 %reduce-scatter.5.cloned.1.call-start = ((), (), s32[]{:S(2)}) async-start(), calls=%async_computation.3 | async-start | bytes 11698176 | tf_op jit(solution)/shard_map/reduce_scatter | solution.py:246
  161.4 13.3 %collective-permute-start.5 = (bf16[2,512,512]{2,1,0:T(8,128)(2,1)S(1)}, bf16[2,512,512]{2,1,0:T(8,128)(2,1)S(1)}, u32[]{:S(2)}, u32[]{:S(2)}) collective-permute-start(bf16[2,512,512]{2,1,0:T(8,128)(2,1)S(1)} %get-tuple-element.22), channel_id=1, source_target_pairs={{2,0},{4,2},{6,4},{8,6},{10,8},{12,10},{14,12},{16,14},{18,16},{20... | collective-permute-start | bytes 3145736 | tf_op jit(solution)/shard_map/ppermute | solution.py:27
  162.7 54.7 %collective-permute-start.6 = (bf16[2,512,512]{2,1,0:T(8,128)(2,1)S(1)}, bf16[2,512,512]{2,1,0:T(8,128)(2,1)S(1)}, u32[]{:S(2)}, u32[]{:S(2)}) collective-permute-start(bf16[2,512,512]{2,1,0:T(8,128)(2,1)S(1)} %get-tuple-element.21), channel_id=1, source_target_pairs={{4,0},{6,2},{8,4},{10,6},{12,8},{14,10},{16,12},{18,14},{20,16},{2... | collective-permute-start | bytes 3145736 | tf_op jit(solution)/shard_map/ppermute | solution.py:27
  232.3 1.2 copy-start.5
  244.1 20.8 %slice-start.2 = ((s8[5505024]{0:T(1024)(128)(4,1)}), s8[4194304]{0:T(1024)(128)(4,1)S(1)}, s32[]{:S(2)}) async-start(s8[5505024]{0:T(1024)(128)(4,1)} %bitcast.24), calls=%async_computation.6 | async-start | bytes 8388608
  250.2 14.8 %slice-start.3 = ((s8[5505024]{0:T(1024)(128)(4,1)}), s8[1310720]{0:T(1024)(128)(4,1)S(1)}, s32[]{:S(2)}) async-start(s8[5505024]{0:T(1024)(128)(4,1)} %bitcast.24), calls=%async_computation.7 | async-start | bytes 2621440
  250.2 45.7 %collective-permute-start.7 = (bf16[256,5376]{1,0:T(8,128)(2,1)}, bf16[256,5376]{1,0:T(8,128)(2,1)S(1)}, u32[]{:S(2)}, u32[]{:S(2)}) collective-permute-start(bf16[256,5376]{1,0:T(8,128)(2,1)} %fusion.4), channel_id=1, source_target_pairs={{0,1},{1,0},{2,3},{3,2},{4,5},{5,4},{6,7},{7,6},{8,9},{9,8},{10,11... | collective-permute-start | bytes 8257544 | tf_op jit(solution)/shard_map/ppermute | solution.py:32
Sparse Core Ops, SparseCore 0:
  159.8 138.6 reduce-scatter.2
  303.1 122.4 reduce-scatter.4

commit v2 on v1

--- a/solution.py
+++ b/solution.py
@@ -245,7 +245,6 @@
         ).astype(BF16)
         return lax.psum_scatter(partial, "ctx", scatter_dimension=0, tiled=True).astype(F32)
 
-    query_weight_grad = weight_grad(grad_query)
     backs = [
         passed_along(far[:, (reach - distance) * rows : (reach - distance + 1) * rows], "ctx", -distance)
         for distance in range(1, reach + 1)
@@ -273,16 +272,16 @@
         rotated(input_term(lax.rem(me + distance, peers)), "heads", distance)
         for distance in range(1, peers)
     ]
-    pair_weight_grad = weight_grad(jnp.concatenate([grad_key, grad_value], axis=1))
+    summed = weight_grad(jnp.concatenate([grad_query, grad_key, grad_value], axis=1))
     input_sum = input_term(me).astype(F32)
     for term in arrived:
         input_sum += term.astype(F32)
     return (
         attention,
         input_sum.astype(BF16),
-        query_weight_grad,
-        pair_weight_grad[:, :key_width],
-        pair_weight_grad[:, key_width:],
+        summed[:, :query_width],
+        summed[:, query_width : query_width + key_width],
+        summed[:, query_width + key_width :],
     )
 
 

time: 436 us -> 445 us (1.021)
  waiting for transfers between devices: 249 us -> 268 us
  matrix products: 94.2 us -> 86.7 us
    reduce_scatter x2 -> x1, waiting for transfers between devices: 121 us -> 145 us  [weight_grad(): lax.psum_scatter(partial, 'ctx', scatter_dimension=0, tiled=True)]
    ppermute x4, waiting for transfers between devices: 60.8 us -> 53.7 us  [passed_along(): return lax.ppermute(block, axis, route)]
    dot_general x9, matrix products: 30.8 us -> 24.7 us  [dot_nn(): return jnp.dot(a, b, preferred_element_type=F32)]
    dot_general x2 -> x1, matrix products: 23.1 us -> 17.8 us  [weight_grad(): lax.dot_general(tokens, columns, (((0,), (0,)), ((), ())), preferred_elem...]
  transfers between devices with their start and end apart: 10 -> 9, of which waited for: 8 -> 8; matrix products, arithmetic and copies ran while one was open for 20% -> 17% of each run, Pallas kernels for 1% -> 0%
where the time goes in v2:
time: 445 us; the launch traced here: 444 us
  waiting for transfers between devices  268 us (60%)
  matrix products  86.7 us (19%)
  Pallas kernels  37.8 us (8%)
  local copies, waits for them, and re-layouts  20 us (4%)
  starting transfers between devices  14.8 us (3%)
  between operations  14.4 us (3%)
    reduce_scatter x1, waiting for transfers between devices, weight_grad(): lax.psum_scatter(partial, 'ctx', scatter_dimension=0, tiled=True)  145 us
    ppermute x4, waiting for transfers between devices, rotated(): lax.ppermute(block, axis, [(i, (i + distance) % size) for i in range(size)])  68.7 us
    ppermute x4, waiting for transfers between devices, passed_along(): return lax.ppermute(block, axis, route)  53.7 us
    dot_general x6, matrix products, dot_nt(): lax.dot_general(a, b, (((1,), (1,)), ((), ())), preferred_element_type=F32)  44.3 us
    pallas_call x1, Pallas kernels, per_device(): pl.pallas_call(functools.partial(attention_kernel, rows), grid=(kv_heads,...  32.7 us
    dot_general x9, matrix products, dot_nn(): return jnp.dot(a, b, preferred_element_type=F32)  24.7 us
    dot_general x1, matrix products, weight_grad(): lax.dot_general(tokens, columns, (((0,), (0,)), ((), ())), preferred_elem...  17.8 us
  transfers between devices with their start and end apart: 9, of which 8 were waited for; matrix products, arithmetic and copies ran while one was open for 17% of the time, Pallas kernels for 0%

profile of v2, /device:TPU:0, one launch (start us, length us, event | category | flops | bytes accessed | tf_op | source)
XLA Modules:
  0.0 444.2 jit_solution(9794258074434098659)
XLA Ops:
  7.2 0.0 reduce-scatter.2.cloned.1.call-start
  7.2 0.1 broadcast.13.clone
  7.3 3.4 fusion.61
  10.7 3.0 collective-permute-start.2
  13.7 0.0 collective-permute-start.1
  13.7 2.0 collective-permute-start
  15.7 1.4 broadcast.13.clone.2
  17.1 2.3 constant_dynamic-update-slice_fusion.1
  19.4 0.1 broadcast.13.clone.1
  19.5 1.3 constant_dynamic-update-slice_fusion.3
  20.8 1.0 fusion.53
  21.8 0.2 pad_maximum_fusion.1
  22.0 0.0 slice-start.5
  22.0 13.2 %collective-permute-done.2 = bf16[256,1792]{1,0:T(8,128)(2,1)} collective-permute-done((bf16[256,1792]{1,0:T(8,128)(2,1)}, bf16[256,1792]{1,0:T(8,128)(2,1)}, u32[]{:S(2)}, u32[]{:S(2)}) %collective-permute-start.2) | collective-permute-done | bytes 917536 | tf_op jit(solution)/shard_map/ppermute | solution.py:32
  35.2 2.2 constant_dynamic-update-slice_fusion
  37.3 3.3 fusion.21
  40.7 0.0 slice-start.1
  40.7 14.2 %collective-permute-done.1 = bf16[256,1792]{1,0:T(8,128)(2,1)} collective-permute-done((bf16[256,1792]{1,0:T(8,128)(2,1)}, bf16[256,1792]{1,0:T(8,128)(2,1)}, u32[]{:S(2)}, u32[]{:S(2)}) %collective-permute-start.1) | collective-permute-done | bytes 917536 | tf_op jit(solution)/shard_map/ppermute | solution.py:32
  54.8 1.3 constant_dynamic-update-slice_fusion.2
  56.1 0.0 slice-done.4
  56.1 0.0 slice-done.5
  56.1 0.0 copy-start.7
  56.1 1.1 fusion.23
  57.3 2.6 fusion.27
  59.9 1.1 fusion.29
  61.0 12.7 %collective-permute-done = bf16[256,1792]{1,0:T(8,128)(2,1)} collective-permute-done((bf16[256,1792]{1,0:T(8,128)(2,1)}, bf16[256,1792]{1,0:T(8,128)(2,1)}, u32[]{:S(2)}, u32[]{:S(2)}) %collective-permute-start) | collective-permute-done | bytes 917536 | tf_op jit(solution)/shard_map/ppermute | solution.py:32
  73.7 1.3 constant_dynamic-update-slice_fusion.4
  74.9 0.0 copy-start.5
  74.9 1.1 fusion.42.value_ref
  76.1 0.0 copy-start.2
  76.1 1.1 fusion.36.key_ref
  77.2 0.0 copy-start.8
  77.2 1.4 shard_map.110
  78.7 3.7 collective-permute-start.3
  82.3 1.5 collective-permute-start.4
  83.9 4.2 fusion.12
  88.1 0.0 copy-done.5
  88.1 4.1 fusion.14
  92.2 6.0 %add_add_fusion.query_ref = f32[512,1024]{1,0:T(8,128)} fusion(f32[512,1024]{1,0:T(8,128)S(1)} %fusion.14, f32[512,1024]{1,0:T(8,128)S(1)} %fusion.12, bf16[512,1792]{1,0:T(8,128)(2,1)} %constant_dynamic-update-slice_fusion, bf16[5376,1024]{1,0:T(8,128)(2,1)} %param.8), kind=kOutput, calls=%fused_computation.27 | convolution fusion | flops 1880096768 | bytes 11796480 | tf_op jit(solution)/shard_map/dot_general | solution.py:84
  98.2 7.7 %collective-permute-done.3 = bf16[2,512,512]{2,1,0:T(8,128)(2,1)S(1)} collective-permute-done((bf16[2,512,512]{2,1,0:T(8,128)(2,1)S(1)}, bf16[2,512,512]{2,1,0:T(8,128)(2,1)S(1)}, u32[]{:S(2)}, u32[]{:S(2)}) %collective-permute-start.3) | collective-permute-done | bytes 1048608 | tf_op jit(solution)/shard_map/ppermute | solution.py:27
  105.9 0.0 collective-permute-done.4
  105.9 1.7 pad_maximum_fusion.span_ref
  107.6 32.7 %shard_map.111 = (bf16[512,1024]{1,0:T(8,128)(2,1)}, bf16[512,1024]{1,0:T(8,128)(2,1)S(1)}, f32[2,512,512]{2,1,0:T(8,128)S(1)}, bf16[2,1024,512]{2,1,0:T(8,128)(2,1)}) custom-call(s32[1]{0:T(128)} %bitcast.base_ref, f32[512,1024]{1,0:T(8,128)} %add_add_fusion.query_ref, bf16[512,1024]{1,0:T(8,128)(2,1)S(1)} %copy-done.1, ...), custom_call_target="tpu_custom_call" | custom-call | tf_op jit(solution)/shard_map/pallas_call | solution.py:208
  140.4 1.3 copy-done
  141.7 1.7 fusion.62
  143.4 1.3 collective-permute-start.5
  144.7 1.5 collective-permute-start.6
  146.2 10.5 %collective-permute-done.5.rest_0_ = bf16[2,512,512]{2,1,0:T(8,128)(2,1)S(1)} collective-permute-done((bf16[2,512,512]{2,1,0:T(8,128)(2,1)S(1)}, bf16[2,512,512]{2,1,0:T(8,128)(2,1)S(1)}, u32[]{:S(2)}, u32[]{:S(2)}) %collective-permute-start.5) | collective-permute-done | bytes 1048608 | tf_op jit(solution)/shard_map/ppermute | solution.py:27
  156.7 35.5 %collective-permute-done.6.rest_1_ = bf16[2,512,512]{2,1,0:T(8,128)(2,1)S(1)} collective-permute-done((bf16[2,512,512]{2,1,0:T(8,128)(2,1)S(1)}, bf16[2,512,512]{2,1,0:T(8,128)(2,1)S(1)}, u32[]{:S(2)}, u32[]{:S(2)}) %collective-permute-start.6) | collective-permute-done | bytes 1048608 | tf_op jit(solution)/shard_map/ppermute | solution.py:27
  192.2 3.7 shard_map.112
  195.9 17.8 %multiply_convert_fusion = bf16[5376,2048]{1,0:T(8,128)(2,1)} fusion(bf16[512,1792]{1,0:T(8,128)(2,1)} %constant_dynamic-update-slice_fusion, bf16[512,1792]{1,0:T(8,128)(2,1)S(1)} %copy-done.8, bf16[512,1792]{1,0:T(8,128)(2,1)S(1)} %copy-done.6, bf16[512,512]{1,0:T(8,128)(2,1)S(1)} %get-tuple-element.16, bf16[512,512]{1,0:T(8,128)(2,1)S(1)} %get-tuple-element.15, ...), kind=kOutput, calls=%fused_computation | convolution fusion | flops 11319115776 | bytes 29622272 | tf_op jit(solution)/shard_map/dot_general | solution.py:241
  213.6 0.0 reduce-scatter.2.cloned.1.call-update
  213.7 6.0 %fusion.45 = f32[256,5376]{1,0:T(8,128)S(1)} fusion(bf16[5376,1024]{1,0:T(8,128)(2,1)} %param.8, bf16[512,1024]{1,0:T(8,128)(2,1)S(1)} %get-tuple-element.12, s32[]{:T(128)S(6)} %select_n.5), kind=kOutput, calls=%fused_computation.44 | convolution fusion | flops 2818572288 | bytes 17039364 | tf_op jit(solution)/shard_map/dot_general | solution.py:80
  219.7 5.1 %convolution_add_fusion.1 = f32[256,5376]{1,0:T(8,128)S(1)} fusion(f32[256,5376]{1,0:T(8,128)S(1)} %fusion.45, bf16[5376,512]{1,0:T(8,128)(2,1)} %param.9, bf16[512,512]{1,0:T(8,128)(2,1)S(1)} %get-tuple-element.15, s32[]{:T(128)S(6)} %select_n.5), kind=kOutput, calls=%fused_computation.2 | convolution fusion | flops 1410662400 | bytes 16777220 | tf_op jit(solution)/shard_map/dot_general | solution.py:80
  224.8 0.0 slice-start.2
  224.8 7.2 %fusion.4 = bf16[256,5376]{1,0:T(8,128)(2,1)} fusion(f32[256,5376]{1,0:T(8,128)S(1)} %convolution_add_fusion.1, bf16[5376,512]{1,0:T(8,128)(2,1)} %param.10, bf16[512,512]{1,0:T(8,128)(2,1)S(1)} %get-tuple-element.16, s32[]{:T(128)S(6)} %select_n.5), kind=kOutput, calls=%fused_computation.9 | convolution fusion | flops 1412038656 | bytes 14024708 | tf_op jit(solution)/shard_map/dot_general | solution.py:80
  232.0 1.7 collective-permute-start.7
  233.7 15.6 %fusion.47 = f32[256,5376]{1,0:T(8,128)} fusion(bf16[5376,1024]{1,0:T(8,128)(2,1)} %param.8, bf16[512,1024]{1,0:T(8,128)(2,1)S(1)} %get-tuple-element.12, s32[]{:T(128)S(6)} %select_n.4), kind=kOutput, calls=%fused_computation.46 | convolution fusion | flops 2818572288 | bytes 17039364 | tf_op jit(solution)/shard_map/dot_general | solution.py:80
  249.2 4.5 %convolution_add_fusion.3 = f32[256,5376]{1,0:T(8,128)S(1)} fusion(f32[256,5376]{1,0:T(8,128)} %fusion.47, bf16[5376,512]{1,0:T(8,128)(2,1)S(1)} %bitcast.24, bf16[512,512]{1,0:T(8,128)(2,1)S(1)} %get-tuple-element.15, s32[]{:T(128)S(6)} %select_n.4), kind=kOutput, calls=%fused_computation.4 | convolution fusion | flops 1410662400 | bytes 16777220 | tf_op jit(solution)/shard_map/dot_general | solution.py:80
  253.7 28.7 %collective-permute-done.7 = bf16[256,5376]{1,0:T(8,128)(2,1)S(1)} collective-permute-done((bf16[256,5376]{1,0:T(8,128)(2,1)}, bf16[256,5376]{1,0:T(8,128)(2,1)S(1)}, u32[]{:S(2)}, u32[]{:S(2)}) %collective-permute-start.7) | collective-permute-done | bytes 2752544 | tf_op jit(solution)/shard_map/ppermute | solution.py:32
  282.4 5.9 %fusion.3 = bf16[256,5376]{1,0:T(8,128)(2,1)} fusion(f32[256,5376]{1,0:T(8,128)S(1)} %convolution_add_fusion.3, bf16[5376,512]{1,0:T(8,128)(2,1)} %param.10, bf16[256,5376]{1,0:T(8,128)(2,1)S(1)} %collective-permute-done.7, bf16[512,512]{1,0:T(8,128)(2,1)S(1)} %get-tuple-element.16, s32[]{:T(128)S(6)} %select_n.4), kind=kOutput, calls=%fused_computation.8 | convolution fusion | flops 1417543680 | bytes 16777220 | tf_op jit(solution)/shard_map/dot_general | solution.py:80
  288.3 145.3 %reduce-scatter.2.cloned.1.call-done = bf16[336,2048]{1,0:T(8,128)(2,1)} async-done(((bf16[5376,2048]{1,0:T(8,128)(2,1)}), bf16[336,2048]{1,0:T(8,128)(2,1)}) %reduce-scatter.2.cloned.1.call-update) | async-done | bytes 1376272 | tf_op jit(solution)/shard_map/reduce_scatter | solution.py:246
  433.6 2.4 fusion.63
  436.1 1.2 slice.68
  (24 shorter events, 0.1 us)
Async XLA Ops:
  7.2 426.4 %reduce-scatter.2.cloned.1.call-start = ((), (), s32[]{:S(2)}) async-start(), calls=%async_computation.1 | async-start | bytes 23396352 | tf_op jit(solution)/shard_map/reduce_scatter | solution.py:246
  10.7 24.5 %collective-permute-start.2 = (bf16[256,1792]{1,0:T(8,128)(2,1)}, bf16[256,1792]{1,0:T(8,128)(2,1)}, u32[]{:S(2)}, u32[]{:S(2)}) collective-permute-start(bf16[256,1792]{1,0:T(8,128)(2,1)} %get-tuple-element.20), channel_id=1, source_target_pairs={{0,1},{1,0},{2,3},{3,2},{4,5},{5,4},{6,7},{7,6},{8,9},{9,8},{10,11... | collective-permute-start | bytes 2752520 | tf_op jit(solution)/shard_map/ppermute | solution.py:32
  13.7 41.2 %collective-permute-start.1 = (bf16[256,1792]{1,0:T(8,128)(2,1)}, bf16[256,1792]{1,0:T(8,128)(2,1)}, u32[]{:S(2)}, u32[]{:S(2)}) collective-permute-start(bf16[256,1792]{1,0:T(8,128)(2,1)} %get-tuple-element.17), channel_id=1, source_target_pairs={{0,1},{1,0},{2,3},{3,2},{4,5},{5,4},{6,7},{7,6},{8,9},{9,8},{10,11... | collective-permute-start | bytes 2752520 | tf_op jit(solution)/shard_map/ppermute | solution.py:32
  13.7 60.0 %collective-permute-start = (bf16[256,1792]{1,0:T(8,128)(2,1)}, bf16[256,1792]{1,0:T(8,128)(2,1)}, u32[]{:S(2)}, u32[]{:S(2)}) collective-permute-start(bf16[256,1792]{1,0:T(8,128)(2,1)} %get-tuple-element.19), channel_id=1, source_target_pairs={{0,1},{1,0},{2,3},{3,2},{4,5},{5,4},{6,7},{7,6},{8,9},{9,8},{10,11... | collective-permute-start | bytes 2752520 | tf_op jit(solution)/shard_map/ppermute | solution.py:32
  17.1 39.0 %slice-start.4 = ((s8[5505024]{0:T(1024)(128)(4,1)}), s8[1310720]{0:T(1024)(128)(4,1)S(1)}, s32[]{:S(2)}) async-start(s8[5505024]{0:T(1024)(128)(4,1)} %bitcast.25), calls=%async_computation.6 | async-start | bytes 2621440
  22.0 34.1 %slice-start.5 = ((s8[5505024]{0:T(1024)(128)(4,1)}), s8[4194304]{0:T(1024)(128)(4,1)S(1)}, s32[]{:S(2)}) async-start(s8[5505024]{0:T(1024)(128)(4,1)} %bitcast.25), calls=%async_computation.7 | async-start | bytes 8388608
  37.3 19.9 %slice-start = ((s8[5505024]{0:T(1024)(128)(4,1)}), s8[4194304]{0:T(1024)(128)(4,1)S(1)}, s32[]{:S(2)}) async-start(s8[5505024]{0:T(1024)(128)(4,1)} %bitcast.21), calls=%async_computation.2 | async-start | bytes 8388608
  40.7 16.6 %slice-start.1 = ((s8[5505024]{0:T(1024)(128)(4,1)}), s8[1310720]{0:T(1024)(128)(4,1)S(1)}, s32[]{:S(2)}) async-start(s8[5505024]{0:T(1024)(128)(4,1)} %bitcast.21), calls=%async_computation.3 | async-start | bytes 2621440
  56.1 3.8 copy-start.7
  74.9 13.1 %copy-start.5 = (bf16[512,1792]{1,0:T(8,128)(2,1)}, bf16[512,1792]{1,0:T(8,128)(2,1)S(1)}, u32[]{:S(2)}) copy-start(bf16[512,1792]{1,0:T(8,128)(2,1)S(1)} %constant_dynamic-update-slice_fusion.4) | copy-start | bytes 5505028
  76.1 1.1 copy-start.2
  77.2 6.7 %copy-start.8 = (bf16[512,1792]{1,0:T(8,128)(2,1)S(1)}, bf16[512,1792]{1,0:T(8,128)(2,1)}, u32[]{:S(2)}) copy-start(bf16[512,1792]{1,0:T(8,128)(2,1)} %copy-done.7) | copy-start | bytes 5505028
  78.7 27.2 %collective-permute-start.3 = (bf16[2,512,512]{2,1,0:T(8,128)(2,1)S(1)}, bf16[2,512,512]{2,1,0:T(8,128)(2,1)S(1)}, u32[]{:S(2)}, u32[]{:S(2)}) collective-permute-start(bf16[2,512,512]{2,1,0:T(8,128)(2,1)S(1)} %shard_map.110), channel_id=1, source_target_pairs={{0,4},{2,6},{4,8},{6,10},{8,12},{10,14},{12,16},{14,18},{16,20},{1... | collective-permute-start | bytes 3145736 | tf_op jit(solution)/shard_map/ppermute | solution.py:27
  82.3 23.5 %collective-permute-start.4 = (bf16[2,512,512]{2,1,0:T(8,128)(2,1)S(1)}, bf16[2,512,512]{2,1,0:T(8,128)(2,1)S(1)}, u32[]{:S(2)}, u32[]{:S(2)}) collective-permute-start(bf16[2,512,512]{2,1,0:T(8,128)(2,1)S(1)} %shard_map.110), channel_id=1, source_target_pairs={{0,2},{2,4},{4,6},{6,8},{8,10},{10,12},{12,14},{14,16},{16,18},{18... | collective-permute-start | bytes 3145736 | tf_op jit(solution)/shard_map/ppermute | solution.py:27
  98.2 9.4 %copy-start.1 = (bf16[512,1024]{1,0:T(8,128)(2,1)S(1)}, bf16[512,1024]{1,0:T(8,128)(2,1)}, u32[]{:S(2)}) copy-start(bf16[512,1024]{1,0:T(8,128)(2,1)} %out_grad_ref.1) | copy-start | bytes 3145732
  98.2 9.4 %copy-start.3 = (f32[128]{0:T(128)S(1)}, f32[128]{0:T(128)}, u32[]{:S(2)}) copy-start(f32[128]{0:T(128)} %param.11) | copy-start | bytes 1540
  140.4 1.3 copy-start
  143.4 13.3 %collective-permute-start.5 = (bf16[2,512,512]{2,1,0:T(8,128)(2,1)S(1)}, bf16[2,512,512]{2,1,0:T(8,128)(2,1)S(1)}, u32[]{:S(2)}, u32[]{:S(2)}) collective-permute-start(bf16[2,512,512]{2,1,0:T(8,128)(2,1)S(1)} %get-tuple-element.22), channel_id=1, source_target_pairs={{2,0},{4,2},{6,4},{8,6},{10,8},{12,10},{14,12},{16,14},{18,16},{20... | collective-permute-start | bytes 3145736 | tf_op jit(solution)/shard_map/ppermute | solution.py:27
  144.7 47.5 %collective-permute-start.6 = (bf16[2,512,512]{2,1,0:T(8,128)(2,1)S(1)}, bf16[2,512,512]{2,1,0:T(8,128)(2,1)S(1)}, u32[]{:S(2)}, u32[]{:S(2)}) collective-permute-start(bf16[2,512,512]{2,1,0:T(8,128)(2,1)S(1)} %get-tuple-element.21), channel_id=1, source_target_pairs={{4,0},{6,2},{8,4},{10,6},{12,8},{14,10},{16,12},{18,14},{20,16},{2... | collective-permute-start | bytes 3145736 | tf_op jit(solution)/shard_map/ppermute | solution.py:27
  192.2 3.7 copy-start.6
  224.8 24.5 %slice-start.2 = ((s8[5505024]{0:T(1024)(128)(4,1)}), s8[4194304]{0:T(1024)(128)(4,1)S(1)}, s32[]{:S(2)}) async-start(s8[5505024]{0:T(1024)(128)(4,1)} %bitcast.23), calls=%async_computation.4 | async-start | bytes 8388608
  232.0 17.3 %slice-start.3 = ((s8[5505024]{0:T(1024)(128)(4,1)}), s8[1310720]{0:T(1024)(128)(4,1)S(1)}, s32[]{:S(2)}) async-start(s8[5505024]{0:T(1024)(128)(4,1)} %bitcast.23), calls=%async_computation.5 | async-start | bytes 2621440
  232.0 50.4 %collective-permute-start.7 = (bf16[256,5376]{1,0:T(8,128)(2,1)}, bf16[256,5376]{1,0:T(8,128)(2,1)S(1)}, u32[]{:S(2)}, u32[]{:S(2)}) collective-permute-start(bf16[256,5376]{1,0:T(8,128)(2,1)} %fusion.4), channel_id=1, source_target_pairs={{0,1},{1,0},{2,3},{3,2},{4,5},{5,4},{6,7},{7,6},{8,9},{9,8},{10,11... | collective-permute-start | bytes 8257544 | tf_op jit(solution)/shard_map/ppermute | solution.py:32
  433.6 2.5 copy-start.4
Sparse Core Ops, SparseCore 0:
  213.8 219.7 reduce-scatter.1
